TPU v7x, 256 devices: a whole 4x4x8 slice. The times are simulated.
256 devices in a mesh: leaf: 256 (over z, y, x, core).
Axes of the slice: x: 4, y: 4, z: 8, core: 2. Of those that a mesh axis runs over, the one named last changes fastest.
Arguments:
- rhs: float32 [262144, 128], P('leaf'), may hold values from -6 to 6
- proj_bases: float32 [5, 262144, 256], P(None, 'leaf'), may hold values from -6 to 6
- corr_bases: float32 [5, 262144, 256], P(None, 'leaf'), may hold values from -0.375 to 0.375
- cores: float32 [5, 8192, 512], P(None, 'leaf'), may hold values from -0.25 to 0.25
Outputs:
- solution: float32 [262144, 128], P('leaf')
All inputs are finite; a program needn't handle non-finite values.
Results may differ from a plain program's by a relative error of at most 0.00017.
Values sent between devices are 32-bit elements; how exact they have to be, the bound alone decides.
A program may use at most 64 MiB of HBM per device.

v0:
```python
import functools

import jax
import jax.numpy as jnp
from jax import lax
from jax.experimental import pallas as pl
from jax.experimental.pallas import tpu as pltpu
from jax.sharding import PartitionSpec as P

f32, bf16 = jnp.float32, jnp.bfloat16
ROWS, RANK, COLS = 1024, 256, 128
MESH = pl.DeviceIdType.MESH

RING = list(range(1, 8))
XS = [2, 4, 6]
YS = [8, 16, 24]
YZ = [8, 16, 24, 32, 40, 48, 56]
ZS4 = [32, 64, 96]
ZS8 = [32 * k for k in range(1, 8)]
EXCHANGE = {4: [8], 3: YS, 2: YZ, 1: ZS4, 0: ZS8}
GREET = sorted(set(RING + YS + YZ + ZS8))
PIECES = {4: (1, 1, 4, 2, 32, 512), 3: (1, 2, 4, 2, 16, 512), 2: (1, 4, 4, 2, 8, 512),
          1: (2, 4, 4, 2, 8, 256), 0: (4, 4, 4, 2, 8, 128)}

NN = ((1,), (0,))
NT = ((1,), (1,))


def split(a):
    high = a.astype(bf16)
    return high, (a - high.astype(f32)).astype(bf16)


def mm(a, b, dims=NN):
    def one(u, v):
        return lax.dot_general(u, v, (dims, ((), ())), preferred_element_type=f32)
    return one(a[0], b[0]) + (one(a[0], b[1]) + one(a[1], b[0]))


class Sems:
    def __init__(self, send, recv):
        self.send, self.recv, self.used, self.copies = send, recv, 0, []


def kernel(nsem, rhs, proj, corr, cores, out, xin, pin, win, cst, xt, xts, x1, ps, wts, ws0,
           yb, rsb, sb, eb, tb, c4, c3, c2, c1, c0, chl, gloc, grh, gs1, gry, gs2, grx, gfin,
           g34, g23, y1e, outb, lsem, send_sem, recv_sem):
    me = lax.axis_index("leaf")
    h, x = me % 2, (me // 2) % 4
    y, z = (me // 8) % 4, me // 32
    s = me % 8
    cb = {4: c4, 3: c3, 2: c2, 1: c1, 0: c0}
    used = [0]
    everything = []

    def send(src, dst, mask):
        k = used[0]
        used[0] += 1
        copy = pltpu.make_async_remote_copy(
            src_ref=src, dst_ref=dst, send_sem=send_sem.at[k], recv_sem=recv_sem.at[k],
            device_id=(me ^ mask,), device_id_type=MESH)
        copy.start()
        everything.append(copy)
        return copy

    def landed(copies):
        for copy in copies:
            copy.wait_recv()

    nlocal = [0]

    def local(src, dst):
        copy = pltpu.make_async_copy(src, dst, lsem.at[nlocal[0]])
        nlocal[0] += 1
        copy.start()
        return copy

    own = {j: (z % PIECES[j][0], y % PIECES[j][1], x, h) for j in PIECES}
    lx = local(rhs, xin)
    lp, lw = {}, {}
    lp[4] = local(proj.at[4], pin.at[4])
    lc = {}
    for j in (4, 3, 2):
        lc[j] = local(cores.at[j, pl.ds(0, PIECES[j][4])], cb[j].at[own[j]])
    lc[1] = local(cores.at[1, pl.ds(0, 8)], cst.at[1])
    lc[0] = local(cores.at[0, pl.ds(0, 8)], cst.at[0])
    lp[3] = local(proj.at[3], pin.at[3])
    lw[4] = local(corr.at[4], win.at[4])
    for j, k in ((1, 2), (0, 1)):
        lp[j] = local(proj.at[j], pin.at[j])
        lw[k] = local(corr.at[k], win.at[k])
    lp[2] = local(proj.at[2], pin.at[2])
    lw[3] = local(corr.at[3], win.at[3])
    lw[0] = local(corr.at[0], win.at[0])

    barrier = pltpu.get_barrier_semaphore()
    for mask in GREET:
        pl.semaphore_signal(barrier, inc=1, device_id=(me ^ mask,), device_id_type=MESH)

    def ready_p(j):
        lp[j].wait()
        ps[j, 0], ps[j, 1] = split(pin[j])

    def ready_w(k):
        lw[k].wait()
        wts[k - 1, 0], wts[k - 1, 1] = split(win[k].T)

    def p(j):
        return ps[j, 0], ps[j, 1]

    def wt(k):
        return wts[k - 1, 0], wts[k - 1, 1]

    def state():
        return xts[0], xts[1]

    def set_state(value):
        xt[...] = value
        xts[0], xts[1] = split(value)

    def scatter(j):
        return [send(yb.at[j, pl.ds(pl.multiple_of((s ^ m) * 16, 16), 16)], rsb.at[j, m - 1], m)
                for m in RING]

    def ring_sum(j, copies):
        landed(copies)
        total = yb[j, pl.ds(pl.multiple_of(s * 16, 16), 16), :]
        for m in RING:
            total = total + rsb[j, m - 1]
        return total

    def exchange(j, value):
        sb[j] = value
        return [send(sb.at[j], eb.at[j, i], m) for i, m in enumerate(EXCHANGE[j])]

    def small(j, value, copies):
        landed(copies)
        count = len(EXCHANGE[j])
        mine = value
        for i in range(count // 2):
            mine = mine + eb[j, i]
        other = eb[j, count // 2]
        for i in range(count // 2 + 1, count):
            other = other + eb[j, i]
        bit = 7 - j
        left = (me >> bit) % 2 == 0
        scale = (ROWS << bit) ** -0.5
        zl = jnp.where(left, mine, other) * scale
        zr = jnp.where(left, other, mine) * scale
        return mm(split(jnp.concatenate([zl, zr], 1)), (chl[j, 0], chl[j, 1]), NT)

    def gather(j, t):
        rows = pl.ds(pl.multiple_of(s * 16, 16), 16)
        tb[j, rows, :] = t
        return [send(tb.at[j, rows], tb.at[j, rows], m) for m in RING]

    def core_x(j):
        lc[j].wait()
        if j == 1:
            cb[1][own[1]] = jnp.concatenate([cst[1, 0:4, 0:256], cst[1, 0:4, 256:512]], 0)
        if j == 0:
            cb[0][own[0]] = jnp.concatenate(
                [cst[0, 0:2, 128 * k:128 * k + 128] for k in range(4)], 0)
        return [send(cb[j].at[own[j]], cb[j].at[own[j]], m) for m in XS]

    def core_y(j, copies):
        landed(copies)
        view = cb[j].at[own[j][0], own[j][1], :, h]
        return [send(view, view, m) for m in YS[:PIECES[j][1] - 1]]

    def core_z(j, copies):
        landed(copies)
        view = cb[j].at[own[j][0], :, :, h]
        return [send(view, view, m) for m in ZS4[:PIECES[j][0] - 1]]

    def core_swap(j, copies):
        landed(copies)
        view = cb[j].at[:, :, :, h]
        return [send(view, view, 1)]

    def core_done(j, copies):
        landed(copies)
        value = cb[j][...]
        if j >= 2:
            chl[j, 0], chl[j, 1] = split(value.reshape(RANK, 2 * RANK))
            return
        width = PIECES[j][5]
        rows = 4 if j == 1 else 2
        value = value.reshape(RANK // 8, 8 // rows, 8, width)
        for k in range(512 // width):
            part = jnp.concatenate(
                [value[:, q, k * rows:(k + 1) * rows, :] for q in range(8 // rows)], 1)
            chl[j, 0, :, k * width:(k + 1) * width], chl[j, 1, :, k * width:(k + 1) * width] = (
                split(part.reshape(RANK, width)))

    lx.wait()
    set_state(xin[...].T)
    ready_p(4)
    yb[4] = mm(state(), p(4))
    pl.semaphore_wait(barrier, len(GREET))
    scatter4 = scatter(4)
    core4 = core_x(4)

    ready_p(3)
    yb[3] = mm(state(), p(3))
    ready_w(4)
    g34[...] = mm(wt(4), p(3))
    ready_p(1)
    ready_w(2)
    gloc[0] = mm(wt(2), p(1))

    sum4 = ring_sum(4, scatter4)
    exchange4 = exchange(4, sum4)
    core3 = core_x(3)
    core2 = core_x(2)
    core1 = core_x(1)
    core0 = core_x(0)
    ready_p(0)
    gloc[1] = mm(wt(2), p(0))
    core4 = core_swap(4, core4)
    ready_w(1)
    core_done(4, core4)
    t4 = small(4, sum4, exchange4)
    gather4 = gather(4, t4)

    gloc[2] = mm(wt(1), p(0))
    half_mine = pl.ds(pl.multiple_of(h * 128, 128), 128)
    half_other = pl.ds(pl.multiple_of((1 - h) * 128, 128), 128)
    graph = [send(gloc.at[:, half_other], grh, 1)]
    core3 = core_y(3, core3)
    core2 = core_y(2, core2)

    landed(gather4)
    g34s = split(g34[...])
    t4s = split(tb[4])
    yb[3] = yb[3] - mm(t4s, g34s)
    scatter3 = scatter(3)
    set_state(xt[...] - mm(t4s, wt(4)))
    ready_p(2)
    yb[2] = mm(state(), p(2))
    core3 = core_swap(3, core3)
    landed(graph)
    gs1[...] = gloc[:, half_mine, :] + grh[...]
    graph = [send(gs1.at[:, pl.ds(pl.multiple_of((y ^ (m // 8)) * 32, 32), 32)], gry.at[i], m)
             for i, m in enumerate(YS)]
    sum3 = ring_sum(3, scatter3)
    exchange3 = exchange(3, sum3)

    core1 = core_y(1, core1)
    core0 = core_y(0, core0)
    ready_w(3)
    g23[...] = mm(wt(3), p(2))
    core_done(3, core3)
    t3 = small(3, sum3, exchange3)
    gather3 = gather(3, t3)

    core2 = core_swap(2, core2)
    landed(graph)
    mine_y = pl.ds(pl.multiple_of(y * 32, 32), 32)
    gs2[...] = gs1[:, mine_y, :] + gry[0] + gry[1] + gry[2]
    graph = [send(gs2.at[:, pl.ds(pl.multiple_of((x ^ (m // 2)) * 8, 8), 8)], grx.at[i], m)
             for i, m in enumerate(XS)]
    core1 = core_z(1, core1)
    core0 = core_z(0, core0)
    g23s = split(g23[...])

    landed(gather3)
    t3s = split(tb[3])
    yb[2] = yb[2] - mm(t3s, g23s)
    scatter2 = scatter(2)
    set_state(xt[...] - mm(t3s, wt(3)))
    yb[1] = mm(state(), p(1))
    scatter1 = scatter(1)
    yb[0] = mm(state(), p(0))
    scatter0 = scatter(0)
    landed(graph)
    gfin[:, h, y, x] = (gs2[:, pl.ds(pl.multiple_of(x * 8, 8), 8), :]
                        + grx[0] + grx[1] + grx[2])
    graph = [send(gfin.at[:, h, y, x], gfin.at[:, h, y, x], m) for m in XS]
    core_done(2, core2)
    sum2 = ring_sum(2, scatter2)
    exchange2 = exchange(2, sum2)

    def plane_send(j, value):
        sb[j] = value
        return [send(sb.at[j], y1e.at[j, i], m) for i, m in enumerate(YS)]

    def plane_sum(j, value, copies):
        landed(copies)
        return value + y1e[j, 0] + y1e[j, 1] + y1e[j, 2]

    ring1 = ring_sum(1, scatter1)
    plane1 = plane_send(1, ring1)
    landed(graph)
    graph = [send(gfin.at[:, h, y], gfin.at[:, h, y], m) for m in YS]
    ring0 = ring_sum(0, scatter0)
    plane0 = plane_send(0, ring0)
    core1 = core_swap(1, core1)
    core0 = core_swap(0, core0)
    landed(graph)
    graph = [send(gfin.at[:, h], gfin.at[:, h], 1)]
    t2 = small(2, sum2, exchange2)
    t2s = split(t2)
    ring1 = plane_sum(1, ring1, plane1)
    landed(graph)

    def graph_of(g):
        return split(gfin[g].reshape(RANK, RANK))

    ring1 = ring1 - mm(t2s, graph_of(0))
    sb1 = outb
    sb1[0] = ring1
    exchange1 = [send(sb1.at[0], eb.at[1, i], m) for i, m in enumerate(EXCHANGE[1])]
    gather2 = gather(2, t2)
    core_done(1, core1)
    ring0 = plane_sum(0, ring0, plane0)
    ring0 = ring0 - mm(t2s, graph_of(1))
    core_done(0, core0)
    g01s = graph_of(2)
    t1 = small(1, ring1, exchange1)
    ring0 = ring0 - mm(split(t1), g01s)
    sb1[1] = ring0
    exchange0 = [send(sb1.at[1], eb.at[0, i], m) for i, m in enumerate(EXCHANGE[0])]
    gather1 = gather(1, t1)

    landed(gather2)
    set_state(xt[...] - mm(split(tb[2]), wt(2)))
    lw[0].wait()
    ws0[0], ws0[1] = split(win[0])
    landed(gather1)
    x1[...] = (xt[...] - mm(split(tb[1]), wt(1))).T
    t0 = small(0, ring0, exchange0)
    gather0 = gather(0, t0)
    landed(gather0)
    t0s = split(tb[0])
    parts = []
    for k in range(4):
        rows = pl.ds(256 * k, 256)
        x1[rows, :] = x1[rows, :] - mm((ws0[0, rows], ws0[1, rows]), t0s, NT)
        parts.append(local(x1.at[rows], out.at[rows]))
    for copy in everything:
        copy.wait_send()
    for copy in parts:
        copy.wait()
    assert used[0] == nsem, used[0]


NSEM = 145
NLOC = 20


def on_device(rhs, proj_bases, corr_bases, cores):
    any_space = pl.BlockSpec(memory_space=pl.ANY)
    v = pltpu.VMEM
    scratch = [
        v((ROWS, COLS), f32), v((5, ROWS, RANK), f32), v((5, ROWS, RANK), f32), v((2, 8, 512), f32),
        v((COLS, ROWS), f32), v((2, COLS, ROWS), bf16), v((ROWS, COLS), f32),
        v((5, 2, ROWS, RANK), bf16), v((4, 2, RANK, ROWS), bf16), v((2, ROWS, RANK), bf16),
        v((5, COLS, RANK), f32), v((5, 7, 16, RANK), f32), v((5, 16, RANK), f32),
        v((5, 7, 16, RANK), f32), v((5, COLS, RANK), f32),
        v(PIECES[4], f32), v(PIECES[3], f32), v(PIECES[2], f32), v(PIECES[1], f32), v(PIECES[0], f32),
        v((5, 2, RANK, 2 * RANK), bf16),
        v((3, RANK, RANK), f32), v((3, 128, RANK), f32), v((3, 128, RANK), f32),
        v((3, 3, 32, RANK), f32), v((3, 32, RANK), f32), v((3, 3, 8, RANK), f32),
        v((3, 2, 4, 4, 8, RANK), f32),
        v((RANK, RANK), f32), v((RANK, RANK), f32), v((2, 3, 16, RANK), f32), v((2, 16, RANK), f32),
        pltpu.SemaphoreType.DMA((NLOC,)), pltpu.SemaphoreType.DMA((NSEM,)), pltpu.SemaphoreType.DMA((NSEM,)),
    ]
    return pl.pallas_call(
        functools.partial(kernel, NSEM),
        out_shape=jax.ShapeDtypeStruct((ROWS, COLS), f32),
        in_specs=[any_space] * 4,
        out_specs=any_space,
        scratch_shapes=scratch,
        compiler_params=pltpu.CompilerParams(
            collective_id=0, has_side_effects=True, vmem_limit_bytes=56 << 20),
        cost_estimate=pl.CostEstimate(flops=1 << 31, bytes_accessed=12 << 20, transcendentals=0),
    )(rhs, proj_bases, corr_bases, cores)


def solution(mesh):
    return jax.shard_map(
        on_device,
        mesh=mesh,
        in_specs=(
            P("leaf", None),
            P(None, "leaf", None),
            P(None, "leaf", None),
            P(None, "leaf", None),
        ),
        out_specs=P("leaf", None),
        check_vma=False,
    )
```

profile of v0, /device:TPU:1, one launch (start us, length us, event | category | flops | bytes accessed | tf_op | source)
XLA Modules:
  0.0 75.0 jit_solution(5861690940616290456)
XLA Ops:
  0.0 73.1 %shard_map.46 = f32[1024,128]{1,0:T(8,128)} custom-call(f32[1024,128]{1,0:T(8,128)} %rhs.1, f32[5,1024,256]{2,1,0:T(8,128)} %proj.1, f32[5,1024,256]{2,1,0:T(8,128)} %corr.1, f32[5,32,512]{2,1,0:T(8,128)} %cores.1), custom_call_target="tpu_custom_call" | custom-call | flops 2147483648 | bytes 12582912 | tf_op jit(solution)/shard_map/pallas_call | solution.py:369
  73.1 1.9 %copy.6 = f32[1024,128]{1,0:T(8,128)} copy(f32[1024,128]{1,0:T(8,128)} %shard_map.46) | data formatting | bytes 1048576
where the time goes:
time: 75.1 us; the launch traced here: 75 us
  Pallas kernels  73.1 us (97%)
  local copies, waits for them, and re-layouts  1.87 us (2%)
    pallas_call x1, Pallas kernels, on_device(): pl.pallas_call(functools.partial(kernel, NSEM), out_shape=jax.ShapeDtypeS...  73.1 us
    unnamed x1, local copies, waits for them, and re-layouts  1.87 us

commit v1 on v0

--- a/solution.py
+++ b/solution.py
@@ -37,14 +37,10 @@
     return one(a[0], b[0]) + (one(a[0], b[1]) + one(a[1], b[0]))
 
 
-class Sems:
-    def __init__(self, send, recv):
-        self.send, self.recv, self.used, self.copies = send, recv, 0, []
-
-
 def kernel(nsem, rhs, proj, corr, cores, out, xin, pin, win, cst, xt, xts, x1, ps, wts, ws0,
-           yb, rsb, sb, eb, tb, c4, c3, c2, c1, c0, chl, gloc, grh, gs1, gry, gs2, grx, gfin,
-           g34, g23, y1e, outb, lsem, send_sem, recv_sem):
+           yb, rsb, sb, eb, tb, c4, c3, c2, c1, c0, chl, g34, gloc, grh, gs1, gs2,
+           rx23, rx13, rx03, gf23, gf13, gf03, py12, py0, px12, px0, pf12, pf0, y1e,
+           lsem, send_sem, recv_sem):
     me = lax.axis_index("leaf")
     h, x = me % 2, (me // 2) % 4
     y, z = (me // 8) % 4, me // 32
@@ -76,22 +72,30 @@
         return copy
 
     own = {j: (z % PIECES[j][0], y % PIECES[j][1], x, h) for j in PIECES}
+    lp, lw, lc = {}, {}, {}
+
+    def fetch_p(j):
+        lp[j] = local(proj.at[j], pin.at[j])
+
+    def fetch_w(k):
+        lw[k] = local(corr.at[k], win.at[k])
+
     lx = local(rhs, xin)
-    lp, lw = {}, {}
-    lp[4] = local(proj.at[4], pin.at[4])
-    lc = {}
-    for j in (4, 3, 2):
-        lc[j] = local(cores.at[j, pl.ds(0, PIECES[j][4])], cb[j].at[own[j]])
+    fetch_p(4)
+    lc[4] = local(cores.at[4, pl.ds(0, 32)], c4.at[own[4]])
+    fetch_p(1)
+    fetch_w(2)
+    fetch_p(0)
+    fetch_w(1)
+    fetch_p(2)
+    fetch_w(3)
+    lc[3] = local(cores.at[3, pl.ds(0, 16)], c3.at[own[3]])
+    lc[2] = local(cores.at[2, pl.ds(0, 8)], c2.at[own[2]])
     lc[1] = local(cores.at[1, pl.ds(0, 8)], cst.at[1])
     lc[0] = local(cores.at[0, pl.ds(0, 8)], cst.at[0])
-    lp[3] = local(proj.at[3], pin.at[3])
-    lw[4] = local(corr.at[4], win.at[4])
-    for j, k in ((1, 2), (0, 1)):
-        lp[j] = local(proj.at[j], pin.at[j])
-        lw[k] = local(corr.at[k], win.at[k])
-    lp[2] = local(proj.at[2], pin.at[2])
-    lw[3] = local(corr.at[3], win.at[3])
-    lw[0] = local(corr.at[0], win.at[0])
+    fetch_p(3)
+    fetch_w(4)
+    fetch_w(0)
 
     barrier = pltpu.get_barrier_semaphore()
     for mask in GREET:
@@ -130,8 +134,8 @@
         return total
 
     def exchange(j, value):
-        sb[j] = value
-        return [send(sb.at[j], eb.at[j, i], m) for i, m in enumerate(EXCHANGE[j])]
+        sb[2 + j] = value
+        return [send(sb.at[2 + j], eb.at[j, i], m) for i, m in enumerate(EXCHANGE[j])]
 
     def small(j, value, copies):
         landed(copies)
@@ -193,6 +197,72 @@
             chl[j, 0, :, k * width:(k + 1) * width], chl[j, 1, :, k * width:(k + 1) * width] = (
                 split(part.reshape(RANK, width)))
 
+    half_mine = pl.ds(pl.multiple_of(h * 128, 128), 128)
+    half_other = pl.ds(pl.multiple_of((1 - h) * 128, 128), 128)
+
+    def graph_swap(span):
+        return [send(gloc.at[span, half_other], grh.at[span], 1)]
+
+    def chip_sum(span, copies):
+        landed(copies)
+        gs1[span] = gloc[span, half_mine, :] + grh[span]
+
+    def piece(m, unit, size):
+        at = x if unit == 2 else y
+        return pl.ds(pl.multiple_of((at ^ (m // unit)) * size, size), size)
+
+    def ring_scatter(span, copies, got):
+        chip_sum(span, copies)
+        return [send(gs1.at[span, piece(m, 2, 32)], got.at[i], m) for i, m in enumerate(XS)]
+
+    def ring_gather(span, copies, got, full):
+        landed(copies)
+        full[:, h, x] = gs1[span, piece(0, 2, 32), :] + got[0] + got[1] + got[2]
+        view = full.at[:, h, x]
+        return [send(view, view, m) for m in XS]
+
+    def plane_scatter_y(span, copies, got):
+        chip_sum(span, copies)
+        return [send(gs1.at[span, piece(m, 8, 32)], got.at[i], m) for i, m in enumerate(YS)]
+
+    def plane_scatter_x(span, copies, got, got_x):
+        landed(copies)
+        gs2[span] = gs1[span, piece(0, 8, 32), :] + got[0] + got[1] + got[2]
+        return [send(gs2.at[span, piece(m, 2, 8)], got_x.at[i], m) for i, m in enumerate(XS)]
+
+    def plane_gather_x(span, copies, got_x, full):
+        landed(copies)
+        full[:, h, y, x] = gs2[span, piece(0, 2, 8), :] + got_x[0] + got_x[1] + got_x[2]
+        view = full.at[:, h, y, x]
+        return [send(view, view, m) for m in XS]
+
+    def plane_gather_y(copies, full):
+        landed(copies)
+        view = full.at[:, h, y]
+        return [send(view, view, m) for m in YS]
+
+    def full_swap(copies, full):
+        landed(copies)
+        view = full.at[:, h]
+        return [send(view, view, 1)]
+
+    def whole(full, g):
+        return split(full[g].reshape(RANK, RANK))
+
+    def plane_send(j, value):
+        sb[j] = value
+        return [send(sb.at[j], y1e.at[j, i], m) for i, m in enumerate(YS)]
+
+    def plane_sum(j, value, copies):
+        landed(copies)
+        return value + y1e[j, 0] + y1e[j, 1] + y1e[j, 2]
+
+    def exchange_up(j, value):
+        sb[2 + j] = value
+        return [send(sb.at[2 + j], eb.at[j, i], m) for i, m in enumerate(EXCHANGE[j])]
+
+    S12, S0, S23, S13, S03 = (pl.ds(0, 1), pl.ds(1, 2), pl.ds(3, 1), pl.ds(4, 1), pl.ds(5, 1))
+
     lx.wait()
     set_state(xin[...].T)
     ready_p(4)
@@ -201,136 +271,132 @@
     scatter4 = scatter(4)
     core4 = core_x(4)
 
-    ready_p(3)
-    yb[3] = mm(state(), p(3))
-    ready_w(4)
-    g34[...] = mm(wt(4), p(3))
     ready_p(1)
     ready_w(2)
     gloc[0] = mm(wt(2), p(1))
-
+    plane12 = graph_swap(S12)
+    ready_p(0)
+    gloc[1] = mm(wt(2), p(0))
+    ready_w(1)
+    gloc[2] = mm(wt(1), p(0))
     sum4 = ring_sum(4, scatter4)
     exchange4 = exchange(4, sum4)
     core3 = core_x(3)
     core2 = core_x(2)
     core1 = core_x(1)
     core0 = core_x(0)
-    ready_p(0)
-    gloc[1] = mm(wt(2), p(0))
+    plane0s = graph_swap(S0)
+    plane12 = plane_scatter_y(S12, plane12, py12)
+    ready_p(2)
+    ready_w(3)
+    gloc[3] = mm(wt(3), p(2))
+    ring23 = graph_swap(S23)
     core4 = core_swap(4, core4)
-    ready_w(1)
+    gloc[4] = mm(wt(3), p(1))
+    ring13 = graph_swap(S13)
     core_done(4, core4)
     t4 = small(4, sum4, exchange4)
     gather4 = gather(4, t4)
 
-    gloc[2] = mm(wt(1), p(0))
-    half_mine = pl.ds(pl.multiple_of(h * 128, 128), 128)
-    half_other = pl.ds(pl.multiple_of((1 - h) * 128, 128), 128)
-    graph = [send(gloc.at[:, half_other], grh, 1)]
+    ready_p(3)
+    ring23 = ring_scatter(S23, ring23, rx23)
+    yb[3] = mm(state(), p(3))
+    ring13 = ring_scatter(S13, ring13, rx13)
+    ready_w(4)
+    g34[...] = mm(wt(4), p(3))
+    plane12 = plane_scatter_x(S12, plane12, py12, px12)
     core3 = core_y(3, core3)
+    plane0s = plane_scatter_y(S0, plane0s, py0)
     core2 = core_y(2, core2)
 
+    g34s = split(g34[...])
     landed(gather4)
-    g34s = split(g34[...])
     t4s = split(tb[4])
     yb[3] = yb[3] - mm(t4s, g34s)
     scatter3 = scatter(3)
     set_state(xt[...] - mm(t4s, wt(4)))
-    ready_p(2)
     yb[2] = mm(state(), p(2))
-    core3 = core_swap(3, core3)
-    landed(graph)
-    gs1[...] = gloc[:, half_mine, :] + grh[...]
-    graph = [send(gs1.at[:, pl.ds(pl.multiple_of((y ^ (m // 8)) * 32, 32), 32)], gry.at[i], m)
-             for i, m in enumerate(YS)]
+    scatter2 = scatter(2)
+    ring23 = ring_gather(S23, ring23, rx23, gf23)
+    yb[1] = mm(state(), p(1))
+    scatter1 = scatter(1)
+    plane12 = plane_gather_x(S12, plane12, px12, pf12)
+    yb[0] = mm(state(), p(0))
+    scatter0 = scatter(0)
+    ring13 = ring_gather(S13, ring13, rx13, gf13)
     sum3 = ring_sum(3, scatter3)
     exchange3 = exchange(3, sum3)
 
+    core3 = core_swap(3, core3)
+    gloc[5] = mm(wt(3), p(0))
+    ring03 = graph_swap(S03)
+    ring23 = full_swap(ring23, gf23)
     core1 = core_y(1, core1)
+    core_done(3, core3)
+    plane12 = plane_gather_y(plane12, pf12)
+    ring03 = ring_scatter(S03, ring03, rx03)
+    sum2 = ring_sum(2, scatter2)
+    landed(ring23)
+    g23s = whole(gf23, 0)
+    t3 = small(3, sum3, exchange3)
+    t3s = split(t3)
+
+    sum2 = sum2 - mm(t3s, g23s)
+    exchange2 = exchange(2, sum2)
+    gather3 = gather(3, t3)
+    core2 = core_swap(2, core2)
+    plane0s = plane_scatter_x(S0, plane0s, py0, px0)
     core0 = core_y(0, core0)
-    ready_w(3)
-    g23[...] = mm(wt(3), p(2))
-    core_done(3, core3)
-    t3 = small(3, sum3, exchange3)
-    gather3 = gather(3, t3)
-
-    core2 = core_swap(2, core2)
-    landed(graph)
-    mine_y = pl.ds(pl.multiple_of(y * 32, 32), 32)
-    gs2[...] = gs1[:, mine_y, :] + gry[0] + gry[1] + gry[2]
-    graph = [send(gs2.at[:, pl.ds(pl.multiple_of((x ^ (m // 2)) * 8, 8), 8)], grx.at[i], m)
-             for i, m in enumerate(XS)]
     core1 = core_z(1, core1)
+    ring13 = full_swap(ring13, gf13)
+    ring1 = ring_sum(1, scatter1)
+    landed(ring13)
+    ring1 = ring1 - mm(t3s, whole(gf13, 0))
+    plane1 = plane_send(1, ring1)
+    ring03 = ring_gather(S03, ring03, rx03, gf03)
+    plane12 = full_swap(plane12, pf12)
+    core_done(2, core2)
+    plane0s = plane_gather_x(S0, plane0s, px0, pf0)
     core0 = core_z(0, core0)
-    g23s = split(g23[...])
-
-    landed(gather3)
-    t3s = split(tb[3])
-    yb[2] = yb[2] - mm(t3s, g23s)
-    scatter2 = scatter(2)
-    set_state(xt[...] - mm(t3s, wt(3)))
-    yb[1] = mm(state(), p(1))
-    scatter1 = scatter(1)
-    yb[0] = mm(state(), p(0))
-    scatter0 = scatter(0)
-    landed(graph)
-    gfin[:, h, y, x] = (gs2[:, pl.ds(pl.multiple_of(x * 8, 8), 8), :]
-                        + grx[0] + grx[1] + grx[2])
-    graph = [send(gfin.at[:, h, y, x], gfin.at[:, h, y, x], m) for m in XS]
-    core_done(2, core2)
-    sum2 = ring_sum(2, scatter2)
-    exchange2 = exchange(2, sum2)
-
-    def plane_send(j, value):
-        sb[j] = value
-        return [send(sb.at[j], y1e.at[j, i], m) for i, m in enumerate(YS)]
-
-    def plane_sum(j, value, copies):
-        landed(copies)
-        return value + y1e[j, 0] + y1e[j, 1] + y1e[j, 2]
-
-    ring1 = ring_sum(1, scatter1)
-    plane1 = plane_send(1, ring1)
-    landed(graph)
-    graph = [send(gfin.at[:, h, y], gfin.at[:, h, y], m) for m in YS]
-    ring0 = ring_sum(0, scatter0)
-    plane0 = plane_send(0, ring0)
-    core1 = core_swap(1, core1)
-    core0 = core_swap(0, core0)
-    landed(graph)
-    graph = [send(gfin.at[:, h], gfin.at[:, h], 1)]
+    landed(plane12)
+    g12s = whole(pf12, 0)
     t2 = small(2, sum2, exchange2)
     t2s = split(t2)
-    ring1 = plane_sum(1, ring1, plane1)
-    landed(graph)
-
-    def graph_of(g):
-        return split(gfin[g].reshape(RANK, RANK))
-
-    ring1 = ring1 - mm(t2s, graph_of(0))
-    sb1 = outb
-    sb1[0] = ring1
-    exchange1 = [send(sb1.at[0], eb.at[1, i], m) for i, m in enumerate(EXCHANGE[1])]
+    plane1 = plane_sum(1, ring1, plane1)
+    plane1 = plane1 - mm(t2s, g12s)
+    exchange1 = exchange_up(1, plane1)
+
     gather2 = gather(2, t2)
+    ring03 = full_swap(ring03, gf03)
+    plane0s = plane_gather_y(plane0s, pf0)
+    core1 = core_swap(1, core1)
+    ring0 = ring_sum(0, scatter0)
+    landed(ring03)
+    ring0 = ring0 - mm(t3s, whole(gf03, 0))
+    plane0 = plane_send(0, ring0)
     core_done(1, core1)
-    ring0 = plane_sum(0, ring0, plane0)
-    ring0 = ring0 - mm(t2s, graph_of(1))
-    core_done(0, core0)
-    g01s = graph_of(2)
-    t1 = small(1, ring1, exchange1)
-    ring0 = ring0 - mm(split(t1), g01s)
-    sb1[1] = ring0
-    exchange0 = [send(sb1.at[1], eb.at[0, i], m) for i, m in enumerate(EXCHANGE[0])]
+    core0 = core_swap(0, core0)
+    landed(gather3)
+    set_state(xt[...] - mm(split(tb[3]), wt(3)))
+    plane0s = full_swap(plane0s, pf0)
+    t1 = small(1, plane1, exchange1)
+    plane0 = plane_sum(0, ring0, plane0)
+    landed(plane0s)
+    plane0 = plane0 - mm(t2s, whole(pf0, 0)) - mm(split(t1), whole(pf0, 1))
+    exchange0 = exchange_up(0, plane0)
+
     gather1 = gather(1, t1)
-
     landed(gather2)
     set_state(xt[...] - mm(split(tb[2]), wt(2)))
     lw[0].wait()
     ws0[0], ws0[1] = split(win[0])
+    core_done(0, core0)
     landed(gather1)
     x1[...] = (xt[...] - mm(split(tb[1]), wt(1))).T
-    t0 = small(0, ring0, exchange0)
+    t0 = small(0, plane0, exchange0)
     gather0 = gather(0, t0)
+    for copy in everything[:-7]:
+        copy.wait_send()
     landed(gather0)
     t0s = split(tb[0])
     parts = []
@@ -338,14 +404,14 @@
         rows = pl.ds(256 * k, 256)
         x1[rows, :] = x1[rows, :] - mm((ws0[0, rows], ws0[1, rows]), t0s, NT)
         parts.append(local(x1.at[rows], out.at[rows]))
-    for copy in everything:
+    for copy in everything[-7:]:
         copy.wait_send()
     for copy in parts:
         copy.wait()
     assert used[0] == nsem, used[0]
 
 
-NSEM = 145
+NSEM = 183
 NLOC = 20
 
 
@@ -356,14 +422,18 @@
         v((ROWS, COLS), f32), v((5, ROWS, RANK), f32), v((5, ROWS, RANK), f32), v((2, 8, 512), f32),
         v((COLS, ROWS), f32), v((2, COLS, ROWS), bf16), v((ROWS, COLS), f32),
         v((5, 2, ROWS, RANK), bf16), v((4, 2, RANK, ROWS), bf16), v((2, ROWS, RANK), bf16),
-        v((5, COLS, RANK), f32), v((5, 7, 16, RANK), f32), v((5, 16, RANK), f32),
+        v((5, COLS, RANK), f32), v((5, 7, 16, RANK), f32), v((7, 16, RANK), f32),
         v((5, 7, 16, RANK), f32), v((5, COLS, RANK), f32),
         v(PIECES[4], f32), v(PIECES[3], f32), v(PIECES[2], f32), v(PIECES[1], f32), v(PIECES[0], f32),
         v((5, 2, RANK, 2 * RANK), bf16),
-        v((3, RANK, RANK), f32), v((3, 128, RANK), f32), v((3, 128, RANK), f32),
-        v((3, 3, 32, RANK), f32), v((3, 32, RANK), f32), v((3, 3, 8, RANK), f32),
-        v((3, 2, 4, 4, 8, RANK), f32),
-        v((RANK, RANK), f32), v((RANK, RANK), f32), v((2, 3, 16, RANK), f32), v((2, 16, RANK), f32),
+        v((RANK, RANK), f32), v((6, RANK, RANK), f32), v((6, 128, RANK), f32),
+        v((6, 128, RANK), f32), v((3, 32, RANK), f32),
+        v((3, 1, 32, RANK), f32), v((3, 1, 32, RANK), f32), v((3, 1, 32, RANK), f32),
+        v((1, 2, 4, 32, RANK), f32), v((1, 2, 4, 32, RANK), f32), v((1, 2, 4, 32, RANK), f32),
+        v((3, 1, 32, RANK), f32), v((3, 2, 32, RANK), f32),
+        v((3, 1, 8, RANK), f32), v((3, 2, 8, RANK), f32),
+        v((1, 2, 4, 4, 8, RANK), f32), v((2, 2, 4, 4, 8, RANK), f32),
+        v((2, 3, 16, RANK), f32),
         pltpu.SemaphoreType.DMA((NLOC,)), pltpu.SemaphoreType.DMA((NSEM,)), pltpu.SemaphoreType.DMA((NSEM,)),
     ]
     return pl.pallas_call(

time: 75.1 us -> 67.1 us (0.89)
  Pallas kernels: 73.1 us -> 65.1 us
    pallas_call x1, Pallas kernels: 73.1 us -> 65.1 us  [on_device(): pl.pallas_call(functools.partial(kernel, NSEM), out_shape=jax.ShapeDtypeS...]
where the time goes in v1:
time: 67.1 us; the launch traced here: 67 us
  Pallas kernels  65.1 us (97%)
  local copies, waits for them, and re-layouts  1.87 us (3%)
    pallas_call x1, Pallas kernels, on_device(): pl.pallas_call(functools.partial(kernel, NSEM), out_shape=jax.ShapeDtypeS...  65.1 us
    unnamed x1, local copies, waits for them, and re-layouts  1.87 us

profile of v1, /device:TPU:1, one launch (start us, length us, event | category | flops | bytes accessed | tf_op | source)
XLA Modules:
  0.0 67.0 jit_solution(13149312240505688010)
XLA Ops:
  0.0 65.1 %shard_map.46 = f32[1024,128]{1,0:T(8,128)} custom-call(f32[1024,128]{1,0:T(8,128)} %rhs.1, f32[5,1024,256]{2,1,0:T(8,128)} %proj.1, f32[5,1024,256]{2,1,0:T(8,128)} %corr.1, f32[5,32,512]{2,1,0:T(8,128)} %cores.1), custom_call_target="tpu_custom_call" | custom-call | flops 2147483648 | bytes 12582912 | tf_op jit(solution)/shard_map/pallas_call | solution.py:439
  65.1 1.9 %copy.6 = f32[1024,128]{1,0:T(8,128)} copy(f32[1024,128]{1,0:T(8,128)} %shard_map.46) | data formatting | bytes 1048576

commit v2 on v1

--- a/solution.py
+++ b/solution.py
@@ -38,7 +38,7 @@
 
 
 def kernel(nsem, rhs, proj, corr, cores, out, xin, pin, win, cst, xt, xts, x1, ps, wts, ws0,
-           yb, rsb, sb, eb, tb, c4, c3, c2, c1, c0, chl, g34, gloc, grh, gs1, gs2,
+           yb, rsb, sb, eb, tb, c4, c3, c2, c1, c0, cht, g34, gloc, grh, gs1, gs2,
            rx23, rx13, rx03, gf23, gf13, gf03, py12, py0, px12, px0, pf12, pf0, y1e,
            lsem, send_sem, recv_sem):
     me = lax.axis_index("leaf")
@@ -49,19 +49,24 @@
     used = [0]
     everything = []
 
-    def send(src, dst, mask):
+    def send(parts, total):
         k = used[0]
         used[0] += 1
-        copy = pltpu.make_async_remote_copy(
-            src_ref=src, dst_ref=dst, send_sem=send_sem.at[k], recv_sem=recv_sem.at[k],
-            device_id=(me ^ mask,), device_id_type=MESH)
-        copy.start()
-        everything.append(copy)
-        return copy
-
-    def landed(copies):
-        for copy in copies:
-            copy.wait_recv()
+
+        def describe(src, dst, mask):
+            return pltpu.make_async_remote_copy(
+                src_ref=src, dst_ref=dst, send_sem=send_sem.at[k], recv_sem=recv_sem.at[k],
+                device_id=(me ^ mask,), device_id_type=MESH)
+
+        for part in parts:
+            describe(*part).start()
+        group = describe(total, total, parts[0][2])
+        everything.append(group)
+        return group
+
+    def landed(group):
+        if group is not None:
+            group.wait_recv()
 
     nlocal = [0]
 
@@ -123,8 +128,8 @@
         xts[0], xts[1] = split(value)
 
     def scatter(j):
-        return [send(yb.at[j, pl.ds(pl.multiple_of((s ^ m) * 16, 16), 16)], rsb.at[j, m - 1], m)
-                for m in RING]
+        return send([(yb.at[j, pl.ds(pl.multiple_of((s ^ m) * 16, 16), 16)], rsb.at[j, m - 1], m)
+                     for m in RING], rsb.at[j])
 
     def ring_sum(j, copies):
         landed(copies)
@@ -135,7 +140,8 @@
 
     def exchange(j, value):
         sb[2 + j] = value
-        return [send(sb.at[2 + j], eb.at[j, i], m) for i, m in enumerate(EXCHANGE[j])]
+        return send([(sb.at[2 + j], eb.at[j, i], m) for i, m in enumerate(EXCHANGE[j])],
+                    eb.at[j, pl.ds(0, len(EXCHANGE[j]))])
 
     def small(j, value, copies):
         landed(copies)
@@ -151,12 +157,13 @@
         scale = (ROWS << bit) ** -0.5
         zl = jnp.where(left, mine, other) * scale
         zr = jnp.where(left, other, mine) * scale
-        return mm(split(jnp.concatenate([zl, zr], 1)), (chl[j, 0], chl[j, 1]), NT)
+        return mm(split(jnp.concatenate([zl, zr], 1)), (cht[j, 0], cht[j, 1]))
 
     def gather(j, t):
         rows = pl.ds(pl.multiple_of(s * 16, 16), 16)
         tb[j, rows, :] = t
-        return [send(tb.at[j, rows], tb.at[j, rows], m) for m in RING]
+        return send([(tb.at[j, rows], tb.at[j, rows], m) for m in RING],
+                    tb.at[j, pl.ds(0, 112)])
 
     def core_x(j):
         lc[j].wait()
@@ -165,28 +172,31 @@
         if j == 0:
             cb[0][own[0]] = jnp.concatenate(
                 [cst[0, 0:2, 128 * k:128 * k + 128] for k in range(4)], 0)
-        return [send(cb[j].at[own[j]], cb[j].at[own[j]], m) for m in XS]
+        return send([(cb[j].at[own[j]], cb[j].at[own[j]], m) for m in XS],
+                    cb[j].at[0, 0, pl.ds(0, 3), 0])
 
     def core_y(j, copies):
         landed(copies)
         view = cb[j].at[own[j][0], own[j][1], :, h]
-        return [send(view, view, m) for m in YS[:PIECES[j][1] - 1]]
+        count = PIECES[j][1] - 1
+        return send([(view, view, m) for m in YS[:count]], cb[j].at[0, pl.ds(0, count), :, 0])
 
     def core_z(j, copies):
         landed(copies)
         view = cb[j].at[own[j][0], :, :, h]
-        return [send(view, view, m) for m in ZS4[:PIECES[j][0] - 1]]
+        count = PIECES[j][0] - 1
+        return send([(view, view, m) for m in ZS4[:count]], cb[j].at[pl.ds(0, count), :, :, 0])
 
     def core_swap(j, copies):
         landed(copies)
         view = cb[j].at[:, :, :, h]
-        return [send(view, view, 1)]
+        return send([(view, view, 1)], view)
 
     def core_done(j, copies):
         landed(copies)
         value = cb[j][...]
         if j >= 2:
-            chl[j, 0], chl[j, 1] = split(value.reshape(RANK, 2 * RANK))
+            cht[j, 0], cht[j, 1] = split(value.reshape(RANK, 2 * RANK).T)
             return
         width = PIECES[j][5]
         rows = 4 if j == 1 else 2
@@ -194,14 +204,14 @@
         for k in range(512 // width):
             part = jnp.concatenate(
                 [value[:, q, k * rows:(k + 1) * rows, :] for q in range(8 // rows)], 1)
-            chl[j, 0, :, k * width:(k + 1) * width], chl[j, 1, :, k * width:(k + 1) * width] = (
-                split(part.reshape(RANK, width)))
+            columns = pl.ds(k * width, width)
+            cht[j, 0, columns], cht[j, 1, columns] = split(part.reshape(RANK, width).T)
 
     half_mine = pl.ds(pl.multiple_of(h * 128, 128), 128)
     half_other = pl.ds(pl.multiple_of((1 - h) * 128, 128), 128)
 
     def graph_swap(span):
-        return [send(gloc.at[span, half_other], grh.at[span], 1)]
+        return send([(gloc.at[span, half_other], grh.at[span], 1)], grh.at[span])
 
     def chip_sum(span, copies):
         landed(copies)
@@ -213,45 +223,46 @@
 
     def ring_scatter(span, copies, got):
         chip_sum(span, copies)
-        return [send(gs1.at[span, piece(m, 2, 32)], got.at[i], m) for i, m in enumerate(XS)]
+        return send([(gs1.at[span, piece(m, 2, 32)], got.at[i], m) for i, m in enumerate(XS)], got)
 
     def ring_gather(span, copies, got, full):
         landed(copies)
         full[:, h, x] = gs1[span, piece(0, 2, 32), :] + got[0] + got[1] + got[2]
         view = full.at[:, h, x]
-        return [send(view, view, m) for m in XS]
+        return send([(view, view, m) for m in XS], full.at[:, 0, pl.ds(0, 3)])
 
     def plane_scatter_y(span, copies, got):
         chip_sum(span, copies)
-        return [send(gs1.at[span, piece(m, 8, 32)], got.at[i], m) for i, m in enumerate(YS)]
+        return send([(gs1.at[span, piece(m, 8, 32)], got.at[i], m) for i, m in enumerate(YS)], got)
 
     def plane_scatter_x(span, copies, got, got_x):
         landed(copies)
         gs2[span] = gs1[span, piece(0, 8, 32), :] + got[0] + got[1] + got[2]
-        return [send(gs2.at[span, piece(m, 2, 8)], got_x.at[i], m) for i, m in enumerate(XS)]
+        return send([(gs2.at[span, piece(m, 2, 8)], got_x.at[i], m) for i, m in enumerate(XS)],
+                    got_x)
 
     def plane_gather_x(span, copies, got_x, full):
         landed(copies)
         full[:, h, y, x] = gs2[span, piece(0, 2, 8), :] + got_x[0] + got_x[1] + got_x[2]
         view = full.at[:, h, y, x]
-        return [send(view, view, m) for m in XS]
+        return send([(view, view, m) for m in XS], full.at[:, 0, 0, pl.ds(0, 3)])
 
     def plane_gather_y(copies, full):
         landed(copies)
         view = full.at[:, h, y]
-        return [send(view, view, m) for m in YS]
+        return send([(view, view, m) for m in YS], full.at[:, 0, pl.ds(0, 3)])
 
     def full_swap(copies, full):
         landed(copies)
         view = full.at[:, h]
-        return [send(view, view, 1)]
+        return send([(view, view, 1)], view)
 
     def whole(full, g):
         return split(full[g].reshape(RANK, RANK))
 
     def plane_send(j, value):
         sb[j] = value
-        return [send(sb.at[j], y1e.at[j, i], m) for i, m in enumerate(YS)]
+        return send([(sb.at[j], y1e.at[j, i], m) for i, m in enumerate(YS)], y1e.at[j])
 
     def plane_sum(j, value, copies):
         landed(copies)
@@ -259,7 +270,8 @@
 
     def exchange_up(j, value):
         sb[2 + j] = value
-        return [send(sb.at[2 + j], eb.at[j, i], m) for i, m in enumerate(EXCHANGE[j])]
+        return send([(sb.at[2 + j], eb.at[j, i], m) for i, m in enumerate(EXCHANGE[j])],
+                    eb.at[j, pl.ds(0, len(EXCHANGE[j]))])
 
     S12, S0, S23, S13, S03 = (pl.ds(0, 1), pl.ds(1, 2), pl.ds(3, 1), pl.ds(4, 1), pl.ds(5, 1))
 
@@ -395,7 +407,7 @@
     x1[...] = (xt[...] - mm(split(tb[1]), wt(1))).T
     t0 = small(0, plane0, exchange0)
     gather0 = gather(0, t0)
-    for copy in everything[:-7]:
+    for copy in everything[:-1]:
         copy.wait_send()
     landed(gather0)
     t0s = split(tb[0])
@@ -404,14 +416,14 @@
         rows = pl.ds(256 * k, 256)
         x1[rows, :] = x1[rows, :] - mm((ws0[0, rows], ws0[1, rows]), t0s, NT)
         parts.append(local(x1.at[rows], out.at[rows]))
-    for copy in everything[-7:]:
+    for copy in everything[-1:]:
         copy.wait_send()
     for copy in parts:
         copy.wait()
     assert used[0] == nsem, used[0]
 
 
-NSEM = 183
+NSEM = 57
 NLOC = 20
 
 
@@ -425,7 +437,7 @@
         v((5, COLS, RANK), f32), v((5, 7, 16, RANK), f32), v((7, 16, RANK), f32),
         v((5, 7, 16, RANK), f32), v((5, COLS, RANK), f32),
         v(PIECES[4], f32), v(PIECES[3], f32), v(PIECES[2], f32), v(PIECES[1], f32), v(PIECES[0], f32),
-        v((5, 2, RANK, 2 * RANK), bf16),
+        v((5, 2, 2 * RANK, RANK), bf16),
         v((RANK, RANK), f32), v((6, RANK, RANK), f32), v((6, 128, RANK), f32),
         v((6, 128, RANK), f32), v((3, 32, RANK), f32),
         v((3, 1, 32, RANK), f32), v((3, 1, 32, RANK), f32), v((3, 1, 32, RANK), f32),

time: 67.1 us -> 63.5 us (0.946)
  Pallas kernels: 65.1 us -> 61.5 us
    pallas_call x1, Pallas kernels: 65.1 us -> 61.5 us  [on_device(): pl.pallas_call(functools.partial(kernel, NSEM), out_shape=jax.ShapeDtypeS...]
where the time goes in v2:
time: 63.5 us; the launch traced here: 63.3 us
  Pallas kernels  61.5 us (97%)
  local copies, waits for them, and re-layouts  1.87 us (3%)
    pallas_call x1, Pallas kernels, on_device(): pl.pallas_call(functools.partial(kernel, NSEM), out_shape=jax.ShapeDtypeS...  61.5 us
    unnamed x1, local copies, waits for them, and re-layouts  1.87 us

profile of v2, /device:TPU:1, one launch (start us, length us, event | category | flops | bytes accessed | tf_op | source)
XLA Modules:
  0.0 63.3 jit_solution(8858424865291376500)
XLA Ops:
  0.0 61.5 %shard_map.46 = f32[1024,128]{1,0:T(8,128)} custom-call(f32[1024,128]{1,0:T(8,128)} %rhs.1, f32[5,1024,256]{2,1,0:T(8,128)} %proj.1, f32[5,1024,256]{2,1,0:T(8,128)} %corr.1, f32[5,32,512]{2,1,0:T(8,128)} %cores.1), custom_call_target="tpu_custom_call" | custom-call | flops 2147483648 | bytes 12582912 | tf_op jit(solution)/shard_map/pallas_call | solution.py:451
  61.5 1.9 %copy.6 = f32[1024,128]{1,0:T(8,128)} copy(f32[1024,128]{1,0:T(8,128)} %shard_map.46) | data formatting | bytes 1048576

commit v3 on v2

--- a/solution.py
+++ b/solution.py
@@ -165,27 +165,27 @@
         return send([(tb.at[j, rows], tb.at[j, rows], m) for m in RING],
                     tb.at[j, pl.ds(0, 112)])
 
-    def core_x(j):
+    def core_z(j):
         lc[j].wait()
         if j == 1:
             cb[1][own[1]] = jnp.concatenate([cst[1, 0:4, 0:256], cst[1, 0:4, 256:512]], 0)
-        if j == 0:
+        else:
             cb[0][own[0]] = jnp.concatenate(
                 [cst[0, 0:2, 128 * k:128 * k + 128] for k in range(4)], 0)
-        return send([(cb[j].at[own[j]], cb[j].at[own[j]], m) for m in XS],
-                    cb[j].at[0, 0, pl.ds(0, 3), 0])
+        view, count = cb[j].at[own[j]], PIECES[j][0] - 1
+        return send([(view, view, m) for m in ZS4[:count]], cb[j].at[pl.ds(0, count), 0, 0, 0])
+
+    def core_x(j, copies=None):
+        if copies is None:
+            lc[j].wait()
+        landed(copies)
+        view = cb[j].at[:, own[j][1], x, h]
+        return send([(view, view, m) for m in XS], cb[j].at[:, 0, pl.ds(0, 3), 0])
 
     def core_y(j, copies):
         landed(copies)
-        view = cb[j].at[own[j][0], own[j][1], :, h]
-        count = PIECES[j][1] - 1
-        return send([(view, view, m) for m in YS[:count]], cb[j].at[0, pl.ds(0, count), :, 0])
-
-    def core_z(j, copies):
-        landed(copies)
-        view = cb[j].at[own[j][0], :, :, h]
-        count = PIECES[j][0] - 1
-        return send([(view, view, m) for m in ZS4[:count]], cb[j].at[pl.ds(0, count), :, :, 0])
+        view, count = cb[j].at[:, own[j][1], :, h], PIECES[j][1] - 1
+        return send([(view, view, m) for m in YS[:count]], cb[j].at[:, pl.ds(0, count), :, 0])
 
     def core_swap(j, copies):
         landed(copies)
@@ -282,6 +282,8 @@
     pl.semaphore_wait(barrier, len(GREET))
     scatter4 = scatter(4)
     core4 = core_x(4)
+    core1 = core_z(1)
+    core0 = core_z(0)
 
     ready_p(1)
     ready_w(2)
@@ -295,8 +297,8 @@
     exchange4 = exchange(4, sum4)
     core3 = core_x(3)
     core2 = core_x(2)
-    core1 = core_x(1)
-    core0 = core_x(0)
+    core1 = core_x(1, core1)
+    core0 = core_x(0, core0)
     plane0s = graph_swap(S0)
     plane12 = plane_scatter_y(S12, plane12, py12)
     ready_p(2)
@@ -317,10 +319,12 @@
     ready_w(4)
     g34[...] = mm(wt(4), p(3))
     plane12 = plane_scatter_x(S12, plane12, py12, px12)
+    core2 = core_y(2, core2)
     core3 = core_y(3, core3)
     plane0s = plane_scatter_y(S0, plane0s, py0)
-    core2 = core_y(2, core2)
-
+
+    gloc[5] = mm(wt(3), p(0))
+    ring03 = graph_swap(S03)
     g34s = split(g34[...])
     landed(gather4)
     t4s = split(tb[4])
@@ -340,13 +344,13 @@
     exchange3 = exchange(3, sum3)
 
     core3 = core_swap(3, core3)
-    gloc[5] = mm(wt(3), p(0))
-    ring03 = graph_swap(S03)
     ring23 = full_swap(ring23, gf23)
     core1 = core_y(1, core1)
     core_done(3, core3)
+    core2 = core_swap(2, core2)
     plane12 = plane_gather_y(plane12, pf12)
     ring03 = ring_scatter(S03, ring03, rx03)
+    plane0s = plane_scatter_x(S0, plane0s, py0, px0)
     sum2 = ring_sum(2, scatter2)
     landed(ring23)
     g23s = whole(gf23, 0)
@@ -356,11 +360,9 @@
     sum2 = sum2 - mm(t3s, g23s)
     exchange2 = exchange(2, sum2)
     gather3 = gather(3, t3)
-    core2 = core_swap(2, core2)
-    plane0s = plane_scatter_x(S0, plane0s, py0, px0)
     core0 = core_y(0, core0)
-    core1 = core_z(1, core1)
     ring13 = full_swap(ring13, gf13)
+    plane0s = plane_gather_x(S0, plane0s, px0, pf0)
     ring1 = ring_sum(1, scatter1)
     landed(ring13)
     ring1 = ring1 - mm(t3s, whole(gf13, 0))
@@ -368,8 +370,7 @@
     ring03 = ring_gather(S03, ring03, rx03, gf03)
     plane12 = full_swap(plane12, pf12)
     core_done(2, core2)
-    plane0s = plane_gather_x(S0, plane0s, px0, pf0)
-    core0 = core_z(0, core0)
+    plane0s = plane_gather_y(plane0s, pf0)
     landed(plane12)
     g12s = whole(pf12, 0)
     t2 = small(2, sum2, exchange2)
@@ -380,7 +381,6 @@
 
     gather2 = gather(2, t2)
     ring03 = full_swap(ring03, gf03)
-    plane0s = plane_gather_y(plane0s, pf0)
     core1 = core_swap(1, core1)
     ring0 = ring_sum(0, scatter0)
     landed(ring03)

time: 63.5 us -> 62.1 us (0.978)
  Pallas kernels: 61.5 us -> 60.2 us
    pallas_call x1, Pallas kernels: 61.5 us -> 60.2 us  [on_device(): pl.pallas_call(functools.partial(kernel, NSEM), out_shape=jax.ShapeDtypeS...]
where the time goes in v3:
time: 62.1 us; the launch traced here: 62 us
  Pallas kernels  60.2 us (97%)
  local copies, waits for them, and re-layouts  1.87 us (3%)
    pallas_call x1, Pallas kernels, on_device(): pl.pallas_call(functools.partial(kernel, NSEM), out_shape=jax.ShapeDtypeS...  60.2 us
    unnamed x1, local copies, waits for them, and re-layouts  1.87 us

profile of v3, /device:TPU:1, one launch (start us, length us, event | category | flops | bytes accessed | tf_op | source)
XLA Modules:
  0.0 62.0 jit_solution(1403413355342298003)
XLA Ops:
  0.0 60.2 %shard_map.46 = f32[1024,128]{1,0:T(8,128)} custom-call(f32[1024,128]{1,0:T(8,128)} %rhs.1, f32[5,1024,256]{2,1,0:T(8,128)} %proj.1, f32[5,1024,256]{2,1,0:T(8,128)} %corr.1, f32[5,32,512]{2,1,0:T(8,128)} %cores.1), custom_call_target="tpu_custom_call" | custom-call | flops 2147483648 | bytes 12582912 | tf_op jit(solution)/shard_map/pallas_call | solution.py:451
  60.2 1.9 %copy.6 = f32[1024,128]{1,0:T(8,128)} copy(f32[1024,128]{1,0:T(8,128)} %shard_map.46) | data formatting | bytes 1048576

commit v4 on v3

--- a/solution.py
+++ b/solution.py
@@ -311,6 +311,7 @@
     core_done(4, core4)
     t4 = small(4, sum4, exchange4)
     gather4 = gather(4, t4)
+    plane0s = plane_scatter_y(S0, plane0s, py0)
 
     ready_p(3)
     ring23 = ring_scatter(S23, ring23, rx23)
@@ -321,7 +322,6 @@
     plane12 = plane_scatter_x(S12, plane12, py12, px12)
     core2 = core_y(2, core2)
     core3 = core_y(3, core3)
-    plane0s = plane_scatter_y(S0, plane0s, py0)
 
     gloc[5] = mm(wt(3), p(0))
     ring03 = graph_swap(S03)

time: 62.1 us -> 62.2 us (level)
  no operation moved by 1% of the time
where the time goes in v4:
time: 62.2 us; the launch traced here: 62 us
  Pallas kernels  60.2 us (97%)
  local copies, waits for them, and re-layouts  1.87 us (3%)
    pallas_call x1, Pallas kernels, on_device(): pl.pallas_call(functools.partial(kernel, NSEM), out_shape=jax.ShapeDtypeS...  60.2 us
    unnamed x1, local copies, waits for them, and re-layouts  1.87 us

profile of v4, /device:TPU:1, one launch (start us, length us, event | category | flops | bytes accessed | tf_op | source)
XLA Modules:
  0.0 62.0 jit_solution(15396116061951626964)
XLA Ops:
  0.0 60.2 %shard_map.46 = f32[1024,128]{1,0:T(8,128)} custom-call(f32[1024,128]{1,0:T(8,128)} %rhs.1, f32[5,1024,256]{2,1,0:T(8,128)} %proj.1, f32[5,1024,256]{2,1,0:T(8,128)} %corr.1, f32[5,32,512]{2,1,0:T(8,128)} %cores.1), custom_call_target="tpu_custom_call" | custom-call | flops 2147483648 | bytes 12582912 | tf_op jit(solution)/shard_map/pallas_call | solution.py:451
  60.2 1.9 %copy.6 = f32[1024,128]{1,0:T(8,128)} copy(f32[1024,128]{1,0:T(8,128)} %shard_map.46) | data formatting | bytes 1048576
